TPU v7x, 32 devices: a whole 2x2x4 slice. The times are simulated.
32 devices in a mesh: dp: 8 (over y, x, core), mp: 4 (over z).
Axes of the slice: x: 2, y: 2, z: 4, core: 2. Of those that a mesh axis runs over, the one named last changes fastest.
Arguments:
- tokens_in: bfloat16 [16384, 768], P('dp'), may hold values from -6 to 6
- cotangent: bfloat16 [16384, 768], P('dp'), may hold values from -6 to 6
- patch_counts: int32 [16, 10], P('dp'), may hold values from 0 to 100, as said below
- w_qkv: float32 [768, 3, 768], P('dp', None, 'mp'), may hold values from -1 to 1
- w_out: float32 [768, 768], P('mp', 'dp'), may hold values from -0.4375 to 0.4375
- w_up: float32 [768, 3072], P('dp', 'mp'), may hold values from -0.21875 to 0.21875
- w_down: float32 [3072, 768], P('mp', 'dp'), may hold values from -0.109375 to 0.109375
- layer_vector_rows: float32 [8, 768], replicated, may hold values from -1.2 to 2.4
- inner_biases: float32 [6, 768], replicated, may hold values from -3 to 3
- qkvrows_prior: float32 [768], P('dp'), may hold values from 1638 to 6553
- qkvcols_prior: float32 [3, 768], P(None, 'mp'), may hold values from 1638 to 6553
- outrows_prior: float32 [768], P('mp'), may hold values from 2293 to 9175
- outcols_prior: float32 [768], P('dp'), may hold values from 2293 to 9175
- uprows_prior: float32 [768], P('dp'), may hold values from 819 to 3276
- upcols_prior: float32 [3072], P('mp'), may hold values from 819 to 3276
- downrows_prior: float32 [3072], P('mp'), may hold values from 2293 to 9175
- downcols_prior: float32 [768], P('dp'), may hold values from 2293 to 9175
- vector_moment: float32 [8, 768], replicated, may hold values from 1638 to 8192
- bias_moment: float32 [6, 768], replicated, may hold values from 292 to 4681
Outputs:
- stream_out: bfloat16 [16384, 768], P('dp')
- input_grad: float32 [16384, 768], P('dp', 'mp')
- qkv_grad: float32 [768, 3, 768], P('dp', None, 'mp')
- out_grad: float32 [768, 768], P('mp', 'dp')
- up_grad: float32 [768, 3072], P('dp', 'mp')
- down_grad: float32 [3072, 768], P('mp', 'dp')
- qkv_after: float32 [768, 3, 768], P('dp', None, 'mp')
- out_after: float32 [768, 768], P('mp', 'dp')
- up_after: float32 [768, 3072], P('dp', 'mp')
- down_after: float32 [3072, 768], P('mp', 'dp')
- qkv_bfloat: bfloat16 [768, 3, 768], P('dp', None, 'mp')
- out_bfloat: bfloat16 [768, 768], P('mp', 'dp')
- up_bfloat: bfloat16 [768, 3072], P('dp', 'mp')
- down_bfloat: bfloat16 [3072, 768], P('mp', 'dp')
- qkvrows_after: float32 [768], P('dp')
- qkvcols_after: float32 [3, 768], P(None, 'mp')
- outrows_after: float32 [768], P('mp')
- outcols_after: float32 [768], P('dp')
- uprows_after: float32 [768], P('dp')
- upcols_after: float32 [3072], P('mp')
- downrows_after: float32 [3072], P('mp')
- downcols_after: float32 [768], P('dp')
- vector_grad: float32 [8, 768], replicated
- bias_grad: float32 [6, 768], replicated
- moment_vectors: float32 [8, 768], replicated
- moment_biases: float32 [6, 768], replicated
- vectors_after: float32 [8, 768], replicated
- biases_after: float32 [6, 768], replicated
- update_scale: float32 [4], replicated
- token_spread: float32 [3], replicated
Inputs may be any that keep to these rules, and one draw needn't show every extreme that they name: `patch_counts`: every set holds at least one image; used slots come first and hold 60 to 100 patches, the first slot of every set exactly 100; later slots hold 0.
All inputs are finite; a program needn't handle non-finite values.
Results may differ from a plain program's by a relative error of at most 0.018.
Values may be sent and summed in bfloat16 or wider, within the bound.
A program may use at most 192 MiB of HBM per device.

v0:
```python
import functools

import jax
import jax.numpy as jnp
from jax import lax
from jax.experimental import pallas as pl
from jax.experimental.pallas import tpu as pltpu
from jax.sharding import PartitionSpec as P

HD = 64
FF = 3072
STEP = 3


norm_eps = 1e-06
square_eps = 1e-30
clip_limit = 0.5
step_rate = 0.6
mask_fill = -1000000000.0


MESH = pl.DeviceIdType.MESH
HALO = 128
GROUPS = 3

def neighbours(dp):
    core = dp % 2
    return dp + 1 - 2 * core, dp + 2 - 4 * ((dp // 2) % 2), (dp + 4) % 8, (dp + 4) % 8 + 2 - 4 * ((dp // 2) % 2)


def flip(dp):
    return dp + 1 - 2 * (dp % 2)


def greet(devices, extra):
    barrier = pltpu.get_barrier_semaphore()
    for device in devices:
        pl.semaphore_signal(barrier, inc=1, device_id=device, device_id_type=MESH)
    for condition, device in extra:

        @pl.when(condition)
        def _():
            pl.semaphore_signal(barrier, inc=1, device_id=device, device_id_type=MESH)

    peers = len(devices)
    for condition, _ in extra:
        peers = peers + jnp.where(condition, 1, 0)
    pl.semaphore_wait(barrier, peers)


A_Z, A_X, A_Y, A_D0, A_D1, A_S, A_SX, A_SY, A_SD0, A_SD1 = range(10)
KINDS = 10
ORDERS = ((0, 1, 2, 3), (1, 0, 2, 3), (2, 3, 1, 0), (3, 2, 1, 0))


def plane_at(mp, unit):
    codes = [sum(plane * 4**i for i, plane in enumerate(order)) for order in ORDERS]
    code = jnp.where(mp == 0, codes[0], jnp.where(mp == 1, codes[1], jnp.where(mp == 2, codes[2], codes[3])))
    power = jnp.where(unit == 0, 1, jnp.where(unit == 1, 4, jnp.where(unit == 2, 16, 64)))
    return (code // power) % 4

class Gather:
    def __init__(self, n_mp, out, send_sems, recv_sems, way_sems):
        self.dp, self.mp, self.n_mp = lax.axis_index("dp"), lax.axis_index("mp"), n_mp
        self.out, self.send_sems, self.recv_sems, self.way_sems = out, send_sems, recv_sems, way_sems
        self.sib, self.xn, self.yn, self.dn = neighbours(self.dp)
        self.rows = out.shape[4]
        self.up, self.down = jnp.minimum(self.mp + 1, n_mp - 1), jnp.maximum(self.mp - 1, 0)
        self.inner = jnp.where((self.mp > 0) & (self.mp < n_mp - 1), 1, 0)
        half = self.rows // 2
        self.all, self.low, self.high = pl.ds(0, self.rows), pl.ds(0, half), pl.ds(half, half)

    def message(self, kind, group, plane, slot, part, device):
        where = self.out.at[group, plane, slot // 2, slot % 2, part]
        return pltpu.make_async_remote_copy(
            src_ref=where,
            dst_ref=where,
            send_sem=self.send_sems.at[group, plane, kind],
            recv_sem=self.recv_sems.at[group, plane, kind],
            device_id=(device, self.mp),
            device_id_type=MESH,
        )

    def along(self, group, plane, way):
        where = self.out.at[group, plane, self.dp // 2, self.dp % 2]
        return pltpu.make_async_remote_copy(
            src_ref=where,
            dst_ref=where,
            send_sem=self.way_sems.at[group, plane, way],
            recv_sem=self.recv_sems.at[group, plane, A_Z],
            device_id=(self.dp, self.down if way else self.up),
            device_id_type=MESH,
        )

    def sends(self, group, plane):
        dp, xn, yn, dn, sib = self.dp, self.xn, self.yn, self.dn, self.sib
        first = [(A_X, dp, self.all, xn), (A_Y, dp, self.all, yn), (A_S, dp, self.all, sib)]
        second = [(A_D0, xn, self.low, yn), (A_SX, xn, self.all, sib), (A_D1, yn, self.high, xn), (A_SY, yn, self.all, sib)]
        third = [(A_SD0, dn, self.low, sib), (A_SD1, dn, self.high, sib)]
        return [
            [functools.partial(self.message, kind, group, plane, *rest) for kind, *rest in part]
            for part in (first, second, third)
        ]

    def unit(self, t):
        rest = t - self.n_mp
        group = jnp.where(rest < 0, 0, 1 + t % 2)
        return group, plane_at(self.mp, jnp.where(rest < 0, t, rest // 2))

    def guarded(self, t, action):
        if isinstance(t, int):
            if 0 <= t < GROUPS * self.n_mp:
                action(*self.unit(t))
            return

        @pl.when((t >= 0) & (t < GROUPS * self.n_mp))
        def _():
            action(*self.unit(t))

    def stage_z(self, t):
        def action(group, plane):
            @pl.when(plane != self.mp)
            def _():
                self.along(group, plane, 0).wait_recv()

            @pl.when((plane <= self.mp) & (self.mp < self.n_mp - 1))
            def _():
                self.along(group, plane, 0).start()

            @pl.when((plane >= self.mp) & (self.mp > 0))
            def _():
                self.along(group, plane, 1).start()

        self.guarded(t, action)

    def stage_a(self, t):
        def action(group, plane):
            for copy in self.sends(group, plane)[0]:
                copy().start()

        self.guarded(t, action)

    def stage_b(self, t):
        def action(group, plane):
            out = self.sends(group, plane)[1]
            self.message(A_X, group, plane, self.xn, self.all, self.xn).wait_recv()
            out[0]().start()
            out[1]().start()
            self.message(A_Y, group, plane, self.yn, self.all, self.yn).wait_recv()
            out[2]().start()
            out[3]().start()

        self.guarded(t, action)

    def stage_c(self, t):
        def action(group, plane):
            out = self.sends(group, plane)[2]
            self.message(A_D0, group, plane, self.dn, self.low, self.yn).wait_recv()
            out[0]().start()
            self.message(A_D1, group, plane, self.dn, self.high, self.xn).wait_recv()
            out[1]().start()

        self.guarded(t, action)

    def stage_d(self, t):
        def action(group, plane):
            for kind, slot, part in (
                (A_S, self.sib, self.all),
                (A_SX, flip(self.xn), self.all),
                (A_SY, flip(self.yn), self.all),
                (A_SD0, flip(self.dn), self.low),
                (A_SD1, flip(self.dn), self.high),
            ):
                self.message(kind, group, plane, slot, part, self.sib).wait_recv()

        self.guarded(t, action)

    def plane(self, u):
        return plane_at(self.mp, u)

    def begin(self):
        for t in (0, 1):
            self.stage_z(t)
            self.stage_a(t)

        @pl.when(self.inner == 1)
        def _():
            self.stage_z(2)

    def step(self, s):
        self.stage_b(s)
        ahead = (2,)
        for more in ahead:
            self.stage_z(s + more + self.inner)
            self.stage_a(s + more)
        self.stage_c(s - 1)

    def finish(self, t):
        def action(group, plane):
            for part in self.sends(group, plane):
                for copy in part:
                    copy().wait_send()

            @pl.when((plane <= self.mp) & (self.mp < self.n_mp - 1))
            def _():
                self.along(group, plane, 0).wait_send()

            @pl.when((plane >= self.mp) & (self.mp > 0))
            def _():
                self.along(group, plane, 1).wait_send()

        self.guarded(t, action)

R_S, R_D0, R_D1, R_X, R_Y, R_UP, R_DOWN = range(7)
R_KINDS = 7
RING = 4


class Scatter:
    def __init__(self, n_mp, blocks, out, bufs, credit, send_sems, recv_sems):
        self.dp, self.mp, self.n_mp = lax.axis_index("dp"), lax.axis_index("mp"), n_mp
        self.blocks, self.out, self.credit = blocks, out, credit
        self.pair_in, self.halves_in, self.x_in, self.y_in, self.z_in = bufs
        self.send_sems, self.recv_sems = send_sems, recv_sems
        self.sib, self.xn, self.yn, self.dn = neighbours(self.dp)
        self.core = self.dp % 2
        self.here, self.at_x, self.at_y, self.at_d = self.dp // 2, self.xn // 2, self.yn // 2, self.dn // 2
        self.up, self.down = jnp.minimum(self.mp + 1, n_mp - 1), jnp.maximum(self.mp - 1, 0)
        rows = out.shape[1]
        self.all, self.low, self.high = pl.ds(0, rows), pl.ds(0, rows // 2), pl.ds(rows // 2, rows // 2)
        self.fed = 2 * n_mp
        self.units = GROUPS * n_mp

    def offered(self, o):
        if isinstance(o, int) and o >= self.fed:
            return 0, plane_at(self.mp, self.units - 1 - o)
        return 2 - o % 2, plane_at(self.mp, o // 2)

    def unit(self, k):
        if isinstance(k, int) and k >= self.fed:
            return 0, plane_at(self.mp, self.units - 1 - k)
        return 2 - k % 2, plane_at(self.mp, self.n_mp - 1 - k // 2)

    def remote(self, kind, group, plane, src, dst, device):
        return pltpu.make_async_remote_copy(
            src_ref=src,
            dst_ref=dst,
            send_sem=self.send_sems.at[group, plane, kind],
            recv_sem=self.recv_sems.at[group, plane, kind],
            device_id=device,
            device_id_type=MESH,
        )

    def pair(self, o, group, plane):
        return self.remote(
            R_S, group, plane, self.blocks.at[group, plane, :, 1 - self.core], self.pair_in.at[o % RING], (self.sib, self.mp)
        )

    def mine(self, group, plane, place, part=None):
        return self.blocks.at[group, plane, place, self.core, self.all if part is None else part]

    def message(self, kind, group, plane):
        mp = self.mp
        if kind == R_D0:
            src, dst = self.mine(group, plane, self.at_d, self.low), self.halves_in.at[group, plane, 0]
            device = (self.xn, mp)
        elif kind == R_D1:
            src, dst = self.mine(group, plane, self.at_d, self.high), self.halves_in.at[group, plane, 1]
            device = (self.yn, mp)
        elif kind == R_X:
            src, dst, device = self.mine(group, plane, self.at_x), self.x_in.at[group, plane], (self.xn, mp)
        elif kind == R_Y:
            src, dst, device = self.mine(group, plane, self.at_y), self.y_in.at[group, plane], (self.yn, mp)
        elif kind == R_UP:
            src, dst, device = self.mine(group, plane, self.here), self.z_in.at[group, plane], (self.dp, self.up)
        else:
            slot = jnp.where(plane == mp - 1, self.n_mp, plane)
            src, dst, device = self.mine(group, plane, self.here), self.z_in.at[group, slot], (self.dp, self.down)
        return self.remote(kind, group, plane, src, dst, device)

    def from_above(self, group, plane):
        slot = jnp.where(plane == self.mp, self.n_mp, plane)
        return slot, self.remote(
            R_DOWN, group, plane, self.mine(group, plane, self.here), self.z_in.at[group, slot], (self.dp, self.down)
        )

    def offer(self, o, group, plane):
        if isinstance(o, int):
            if o >= RING:
                pl.semaphore_wait(self.credit, 1)
        else:

            @pl.when(o >= RING)
            def _():
                pl.semaphore_wait(self.credit, 1)

        self.pair(o, group, plane).start()

    def add_pair(self, o, group, plane):
        self.pair(o, group, plane).wait_recv()
        self.blocks[group, plane, :, self.core] = self.blocks[group, plane, :, self.core] + self.pair_in[o % RING]

        @pl.when(o < self.units - RING)
        def _():
            pl.semaphore_signal(self.credit, inc=1, device_id=(self.sib, self.mp), device_id_type=MESH)

        self.message(R_D0, group, plane).start()
        self.message(R_D1, group, plane).start()

    def add_halves(self, group, plane):
        for kind, place, part, slot in ((R_D0, self.at_y, self.low, 0), (R_D1, self.at_x, self.high, 1)):
            self.message(kind, group, plane).wait_recv()
            where = self.mine(group, plane, place, part)
            where[...] = where[...] + self.halves_in[group, plane, slot]
        self.message(R_X, group, plane).start()
        self.message(R_Y, group, plane).start()

    def add_plane(self, group, plane):
        f32, mp, last = jnp.float32, self.mp, self.n_mp - 1
        self.message(R_X, group, plane).wait_recv()
        self.message(R_Y, group, plane).wait_recv()
        where = self.mine(group, plane, self.here)
        total = (
            where[...].astype(f32) + self.x_in[group, plane].astype(f32) + self.y_in[group, plane].astype(f32)
        )

        @pl.when(plane == mp)
        def _():
            self.out[(group + 2) % 3] = total

        @pl.when(plane != mp)
        def _():
            where[...] = total.astype(jnp.bfloat16)

        @pl.when((plane > mp) & (mp == 0))
        def _():
            self.message(R_UP, group, plane).start()

        @pl.when((plane < mp) & (mp == last))
        def _():
            self.message(R_DOWN, group, plane).start()

    def add_along(self, group, plane):
        f32, mp, last = jnp.float32, self.mp, self.n_mp - 1
        where = self.mine(group, plane, self.here)

        def add():
            where[...] = (where[...].astype(f32) + self.z_in[group, plane].astype(f32)).astype(jnp.bfloat16)

        @pl.when((plane > mp) & (mp > 0))
        def _():
            self.message(R_UP, group, plane).wait_recv()
            add()
            self.message(R_UP, group, plane).start()

        @pl.when((plane < mp) & (mp < last))
        def _():
            self.from_above(group, plane)[1].wait_recv()
            add()
            self.message(R_DOWN, group, plane).start()

        @pl.when((plane == mp) & (mp > 0))
        def _():
            self.message(R_UP, group, plane).wait_recv()
            self.out[(group + 2) % 3] += self.z_in[group, plane].astype(f32)

        @pl.when((plane == mp) & (mp < last))
        def _():
            slot, copy = self.from_above(group, plane)
            copy.wait_recv()
            self.out[(group + 2) % 3] += self.z_in[group, slot].astype(f32)

    def slot(self, k):
        def do(action, j):
            if isinstance(j, int):
                if 0 <= j < self.units:
                    action(*self.unit(j))
                return

            @pl.when(j >= 0)
            def _():
                action(*self.unit(j))

        do(self.add_halves, k)
        do(self.add_plane, k - 1)
        do(self.add_along, k - 2)

    def finish(self):
        def body(t, _):
            group, plane = t // self.n_mp, t % self.n_mp
            self.pair(0, group, plane).wait_send()
            for kind in (R_D0, R_D1, R_X, R_Y):
                self.message(kind, group, plane).wait_send()

            @pl.when(plane > self.mp)
            def _():
                self.message(R_UP, group, plane).wait_send()

            @pl.when(plane < self.mp)
            def _():
                self.message(R_DOWN, group, plane).wait_send()

            return 0

        lax.fori_loop(0, self.units, body, 0)

LANES = 128
NN = (((1,), (0,)), ((), ()))
NT = (((1,), (1,)), ((), ()))
BIG = 2.0**36


def mm(left, right, dims=NN):
    return lax.dot_general(left, right, dims, preferred_element_type=jnp.float32)


def gelu_parts(t):
    k = 1.0 / (1.0 + 0.2316419 * jnp.abs(t))
    series = k * (
        0.319381530 + k * (-0.356563782 + k * (1.781477937 + k * (-1.821255978 + k * 1.330274429)))
    )
    density = 0.3989422804014327 * jnp.exp(-0.5 * t * t)
    tail = density * series
    phi = jnp.where(t >= 0.0, 1.0 - tail, tail)
    return t * phi, phi + t * density


def row_stats(x):
    width = x.shape[1]
    center = x - jnp.sum(x, axis=1, keepdims=True) * (1.0 / width)
    spread = jnp.sum(center * center, axis=1, keepdims=True) * (1.0 / width)
    inverse = lax.rsqrt(spread + norm_eps)
    return center * inverse, inverse


def image_ends(counts_ref, set_index, slots):
    lane = lax.broadcasted_iota(jnp.int32, (8, LANES), 1) % (LANES // 2)
    low = jnp.zeros((8, LANES), jnp.int32)
    high = jnp.zeros((8, LANES), jnp.int32)
    edge = jnp.int32(0)
    for slot in range(slots + 1):
        after = jnp.int32(1 << 20) if slot == slots else edge + counts_ref[set_index, slot]
        low = jnp.where(lane == slot, edge, low)
        high = jnp.where(lane == slot, after, high)
        edge = after if slot < slots else edge
    return low[0:1], high[0:1], edge


def own_row(hidden_half, tile):
    lane = lax.broadcasted_iota(jnp.int32, tile.shape, 1)
    return (lane < LANES // 2) if hidden_half == 0 else (lane >= LANES // 2)


def keep_half(half, tile, other):
    return jnp.where(own_row(half, tile), tile, other)


HEAD_TILES = ((0, 128, 256, 0, 0), (0, 128, 256, 1, 1), (512, 640, 640, 0, 1))
MIX = 384


def make_features(counts_ref, set_index, slots, set_rows, feat_q, feat_k):
    low, high, total = image_ends(counts_ref, set_index, slots)
    step = 256

    def body(i, _):
        at = pl.ds(pl.multiple_of(i * step, step), step)
        row = lax.broadcasted_iota(jnp.int32, (step, LANES), 0) + i * step
        same = (row >= low) & (row < high)
        lane = lax.broadcasted_iota(jnp.int32, (step, LANES), 1) % (LANES // 2)
        feat_k[at] = jnp.where(same, 1.0, 0.0).astype(jnp.bfloat16)
        feat_q[at] = jnp.where(same | (lane > slots), 0.0, -BIG).astype(jnp.bfloat16)
        return 0

    lax.fori_loop(0, set_rows // step, body, 0)
    return total


def attend(m, qkv, mixed, feat_q, feat_k, window_start, window, step):
    keys, values = [], []
    for q_at, k_at, v_at, half, v_half in HEAD_TILES:
        keys.append(keep_half(half, qkv[m, :, k_at : k_at + LANES], feat_k[...]))
        tile = qkv[m, :, v_at : v_at + LANES]
        values.append(keep_half(v_half, tile, jnp.ones_like(tile)))

    def block(i, _):
        at = pl.ds(pl.multiple_of(window_start + i * step, LANES // 2), step)
        outs = []
        for head, (q_at, k_at, v_at, half, v_half) in enumerate(HEAD_TILES):
            query = keep_half(half, qkv[m, at, q_at : q_at + LANES], feat_q[at])
            scores = mm(query, keys[head], NT)
            top = jnp.max(scores, axis=1, keepdims=True)
            weights = jnp.exp2((scores - top) * (HD ** (-0.5) * 1.4426950408889634)).astype(jnp.bfloat16)
            out = mm(weights, values[head])
            outs.append(out / pltpu.roll(out, LANES // 2, 1))
        here = pl.ds(pl.multiple_of(i * step, LANES // 2), step)
        low = jnp.bfloat16
        mixed[m, here, 0:LANES] = keep_half(0, outs[0], outs[1]).astype(low)
        mixed[m, here, LANES : 2 * LANES] = keep_half(1, outs[2], jnp.zeros_like(outs[2])).astype(low)
        return 0

    lax.fori_loop(0, window // step, block, 0)


TN = (((0,), (0,)), ((), ()))


def norm_grad(x, gain, grad):
    width = x.shape[1]
    unit, inverse = row_stats(x)
    e = grad * gain
    mean_e = jnp.sum(e, axis=1, keepdims=True) * (1.0 / width)
    mean_eu = jnp.sum(e * unit, axis=1, keepdims=True) * (1.0 / width)
    return inverse * (e - mean_e - unit * mean_eu), grad * unit


def attend_back(m, qkv, d_mixed, feat_q, feat_k, window_start, window, acc, d_query):
    band = 3 * LANES
    acc[...] = jnp.zeros_like(acc)
    low = jnp.bfloat16
    scale = HD ** (-0.5)

    def block(b, _):
        start = jnp.clip(b - 1, 0, window // LANES - 3) * LANES
        keys_at = pl.ds(pl.multiple_of(start, LANES), band)
        keys_in = pl.ds(pl.multiple_of(window_start + start, LANES), band)
        here = pl.ds(pl.multiple_of(b * LANES, LANES), LANES)
        rows_in = pl.ds(pl.multiple_of(window_start + b * LANES, LANES), LANES)
        f_q, f_k = feat_q[rows_in], feat_k[keys_in]
        got = []
        for head, (q_at, k_at, v_at, half, v_half) in enumerate(HEAD_TILES):
            q_tile = qkv[m, rows_in, q_at : q_at + LANES]
            k_tile = qkv[m, keys_in, k_at : k_at + LANES]
            v_tile = qkv[m, keys_in, v_at : v_at + LANES]
            mix_at = 0 if head < 2 else LANES
            d_tile = d_mixed[here, mix_at : mix_at + LANES]
            d_out = keep_half(v_half, d_tile, jnp.zeros_like(d_tile))
            scores = mm(keep_half(half, k_tile, f_k), keep_half(half, q_tile, f_q), NT)
            top = jnp.max(scores, axis=0, keepdims=True)
            weights = jnp.exp((scores - top) * scale)
            weights = weights * (1.0 / jnp.sum(weights, axis=0, keepdims=True))
            d_weights = mm(v_tile, d_out, NT)
            delta = jnp.sum(d_weights * weights, axis=0, keepdims=True)
            d_scores = (weights * (d_weights - delta)).astype(low)
            d_key = mm(d_scores, keep_half(half, q_tile * scale, jnp.zeros_like(q_tile)))
            d_value = mm(weights.astype(low), d_out)
            d_q = mm(d_scores, keep_half(half, k_tile * scale, jnp.zeros_like(k_tile)), TN)
            got.append((d_q, d_key, d_value))
        acc[keys_at, 0:LANES] += got[0][1] + got[1][1]
        acc[keys_at, LANES : 2 * LANES] += got[0][2] + got[1][2]
        acc[keys_at, 2 * LANES : 3 * LANES] += got[2][1] + got[2][2]
        d_query[here, 0:LANES] = (got[0][0] + got[1][0]).astype(low)
        d_query[here, LANES : 2 * LANES] = got[2][0].astype(low)
        return 0

    lax.fori_loop(0, window // LANES, block, 0)

def tile_rows(i, first=0):
    return pl.ds(pl.multiple_of(first + i * LANES, LANES), LANES)


def column_sum(v):
    return jnp.sum(v, axis=0, keepdims=True)


class Place:
    def __init__(self, set_rows, own_rows):
        self.set_rows, self.own_rows, self.window = set_rows, own_rows, own_rows + HALO
        mp = lax.axis_index("mp")
        per_set = set_rows // own_rows
        self.set_index, part = mp // per_set, mp % per_set
        self.window_start = pl.multiple_of(part * (set_rows - self.window), LANES)
        self.own_start = pl.multiple_of(part * (self.window - own_rows), LANES)
        self.own = pl.ds(self.own_start, own_rows)
        self.own_set = pl.ds(pl.multiple_of(self.window_start + self.own_start, LANES), own_rows)
        self.tiles = self.window // LANES

    def is_own(self, i):
        first = i * LANES
        return jnp.where((first >= self.own_start) & (first < self.own_start + self.own_rows), 1.0, 0.0)

    def valid(self, i, total):
        row = lax.broadcasted_iota(jnp.int32, (LANES, 1), 0) + (self.window_start + i * LANES)
        return jnp.where(row < total, 1.0, 0.0)


def pack_first(qkv, out, packed):
    out_t = out[...].T
    for i in range(3):
        packed[:, i * LANES : (i + 1) * LANES] = qkv[i, :, 0:LANES]
    packed[:, MIX : MIX + LANES] = out_t[:, 0:LANES]
    tails = [qkv[i, :, LANES:] for i in range(3)]
    packed[:, 512:640] = jnp.concatenate([tails[0], out_t[:, LANES:]], axis=1)
    packed[:, 640:768] = jnp.concatenate([tails[1], tails[2]], axis=1)


def pack_lanes(qkv_rows, out_row):
    heads = [row[:, 0:LANES] for row in (*qkv_rows, out_row)]
    q, k, v, o = [row[:, LANES:] for row in (*qkv_rows, out_row)]
    return jnp.concatenate([*heads, q, o, k, v], axis=1)


def unpack_lanes(row):
    at = ((0, 512), (128, 640), (256, 704), (MIX, 576))
    return [jnp.concatenate([row[:, a : a + LANES], row[:, b : b + LANES // 2]], axis=1) for a, b in at]


def pack_biases(biases, packed, n_mp, width):
    f32 = jnp.float32
    share = width // n_mp
    zero = jnp.zeros((1, share), f32)
    for m in range(n_mp):
        part = [biases[r : r + 1, m * share : (m + 1) * share] for r in (0, 1)]
        packed[m : m + 1] = pack_lanes((part[0], zero, part[1]), zero)
    fan = width // share
    source = lax.broadcasted_iota(jnp.int32, (share, width), 0) * fan
    target = lax.broadcasted_iota(jnp.int32, (share, width), 1)
    total = jnp.zeros((n_mp, width), f32)
    for r in range(fan):
        rows = jnp.concatenate(
            [biases[2 + r : 3 + r, m * share : (m + 1) * share] for m in range(n_mp)], axis=0
        )
        move = jnp.where(target == source + r, 1.0, 0.0)
        total = total + lax.dot_general(rows, move, NN, precision=EXACT, preferred_element_type=f32)
    packed[n_mp : 2 * n_mp] = total

DECAY = 1.0 - STEP ** (-0.8)
EXACT = lax.Precision.HIGHEST
SUB_QKV, SUB_OUT, SUB_UP, SUB_DOWN = range(4)


class Exchange:
    def __init__(self, axis, size, bufs, send_sems, recv_sems):
        self.axis, self.size, self.bufs = axis, size, bufs
        self.send_sems, self.recv_sems = send_sems, recv_sems
        self.me = lax.axis_index(axis)

    def copy(self, away):
        peer = (self.me + away) % self.size
        return pltpu.make_async_remote_copy(
            src_ref=self.bufs.at[0],
            dst_ref=self.bufs.at[away],
            send_sem=self.send_sems.at[away],
            recv_sem=self.recv_sems.at[away],
            device_id={self.axis: peer},
            device_id_type=MESH,
        )

    def send(self, value):
        self.bufs[0] = value
        for away in range(1, self.size):
            self.copy(away).start()

    def total(self):
        for away in range(1, self.size):
            self.copy(away).wait_recv()
        total = jnp.zeros(self.bufs.shape[1:], jnp.float32)
        for index in range(self.size):
            away = (self.me - index + self.size) % self.size
            total = total + self.bufs[away]
        return total

    def wait_sends(self):
        for away in range(1, self.size):
            self.copy(away).wait_send()


class Doubling:
    def __init__(self, value, bufs, send_sems, recv_sems):
        self.value, self.bufs, self.send_sems, self.recv_sems = value, bufs, send_sems, recv_sems
        dp, mp = lax.axis_index("dp"), lax.axis_index("mp")
        sib, xn, yn, _ = neighbours(dp)
        self.peers = (
            {"dp": sib}, {"dp": xn}, {"dp": yn}, {"mp": mp + 1 - 2 * (mp % 2)}, {"mp": (mp + 2) % 4}
        )

    def copy(self, i):
        return pltpu.make_async_remote_copy(
            src_ref=self.value.at[i],
            dst_ref=self.bufs.at[i],
            send_sem=self.send_sems.at[i],
            recv_sem=self.recv_sems.at[i],
            device_id=self.peers[i],
            device_id_type=MESH,
        )

    def send(self, i):
        self.copy(i).start()

    def add(self, i):
        self.copy(i).wait_recv()
        self.value[i + 1] = self.value[i] + self.bufs[i]

    def finish(self):
        for i in range(5):
            self.copy(i).wait_send()


def lane_sums(mask, squares):
    return lax.dot_general(mask, squares, NT, precision=EXACT, preferred_element_type=jnp.float32)


def o_lanes(width):
    lane = lax.broadcasted_iota(jnp.int32, (1, width), 1)
    return jnp.where(((lane >= MIX) & (lane < MIX + 128)) | ((lane >= 576) & (lane < 640)), 1.0, 0.0)


def masks_of(width, scale_rows):
    row = lax.broadcasted_iota(jnp.int32, (8, width), 0)
    is_o = o_lanes(width)
    if not isinstance(scale_rows, list):
        scale_rows = [scale_rows[i : i + 1] for i in range(3)]
    up = jnp.where(row == SUB_UP, scale_rows[0], 0.0)
    down = jnp.where(row == SUB_DOWN, scale_rows[1], 0.0)
    first = scale_rows[2]
    mixed = jnp.where(row == SUB_QKV, first * (1.0 - is_o), jnp.where(row == SUB_OUT, first * is_o, 0.0))
    return up, down, mixed


class Factors:
    def __init__(self, reduced, sub_prior, lane_prior, n_dp, swaps):
        self.reduced, self.sub_prior, self.lane_prior = reduced, sub_prior, lane_prior
        self.rows, self.width = reduced.shape[1:]
        self.whole = float(self.rows * n_dp)
        self.early_mp, self.early_dp, self.late_mp, self.late_dp, self.last_mp, self.last_dp = swaps
        self.shares = jnp.zeros((8, self.rows), jnp.float32)
        self.totals = jnp.zeros((8, 1), jnp.float32)

    def send(self, groups, along_mp, along_dp):
        masks = masks_of(self.width, jnp.ones((3, self.width), jnp.float32))
        rows = jnp.zeros((8, self.rows), jnp.float32)
        columns = []
        for group in groups:
            squares = self.reduced[group] * self.reduced[group]
            columns.append(column_sum(squares))
            rows = rows + lane_sums(masks[group], squares)
        along_dp.send(columns[0] if len(columns) == 1 else jnp.concatenate(columns, axis=0))
        along_mp.send(jnp.concatenate([rows, jnp.zeros((8, LANES - self.rows), jnp.float32)], axis=1))
        self.totals = self.totals + jnp.sum(rows, axis=1, keepdims=True)

    def collect(self, groups, along_mp, along_dp, sub_out, lane_out):
        rows, columns = along_mp.total(), along_dp.total()
        row8 = lax.broadcasted_iota(jnp.int32, (8, LANES), 0)
        count = self.whole * jnp.where(row8 == SUB_QKV, 3.0, jnp.where(row8 == SUB_OUT, 1.0, 4.0))
        sub_new = DECAY * self.sub_prior[...] + (1.0 - DECAY) * (rows / count + square_eps)
        mine = (row8 == SUB_UP) | (row8 == SUB_DOWN)
        if 2 in groups:
            mine = (row8 == SUB_QKV) | (row8 == SUB_OUT)
        sub_out[...] = jnp.where(mine, sub_new, sub_out[...])
        scale_rows = []
        for i, group in enumerate(groups):
            new = DECAY * self.lane_prior[group : group + 1] + (1.0 - DECAY) * (
                columns[i : i + 1] / self.whole + square_eps
            )
            lane_out[group : group + 1] = new
            scale_rows.append(1.0 / new)
        if len(scale_rows) == 1:
            scale_rows = [scale_rows[0]] * 3
        masks = masks_of(self.width, scale_rows + scale_rows[:1])
        shares = jnp.zeros((8, self.rows), jnp.float32)
        for group in groups:
            shares = shares + lane_sums(masks[group], self.reduced[group] * self.reduced[group])
        self.shares = self.shares + jnp.where(mine[:, 0 : self.rows], shares / sub_new[:, 0 : self.rows], 0.0)

    def finish(self, masters, scalar_out):
        f32 = jnp.float32
        masks = masks_of(self.width, jnp.ones((3, self.width), f32))
        weights = jnp.zeros((8, 1), f32)
        for group in range(GROUPS):
            by_lane = column_sum(masters[group] * masters[group])
            weights = weights + jnp.sum(masks[group] * by_lane, axis=1, keepdims=True)
        row1 = lax.broadcasted_iota(jnp.int32, (8, 1), 0)
        lane8 = lax.broadcasted_iota(jnp.int32, (8, LANES), 1)
        sub = jnp.sum(jnp.where(lane8 < self.rows, self.sub_prior[...], 0.0), axis=1, keepdims=True)
        out = jnp.sum(self.lane_prior[2:3] * o_lanes(self.width), axis=1, keepdims=True)
        down = jnp.sum(self.lane_prior[1:2], axis=1, keepdims=True)
        prior = jnp.where(row1 == SUB_OUT, out, jnp.where(row1 == SUB_DOWN, down, sub))
        shares = jnp.sum(self.shares, axis=1, keepdims=True)
        value = jnp.where(
            lane8 == 0, shares, jnp.where(lane8 == 1, weights, jnp.where(lane8 == 2, self.totals, prior))
        )
        self.last_mp.send(value)
        self.last_dp.send(self.last_mp.total())
        scalar_out[...] = self.last_dp.total()

    def wait_sends(self):
        for swap in (self.early_mp, self.early_dp, self.late_mp, self.late_dp, self.last_mp, self.last_dp):
            swap.wait_sends()


def update_kernel(
    n_dp, n_mp, reduced, masters, sub_new, lane_new, scalars, sums, vec, bias, vec_moment, bias_moment, input_in, stream_in,
    stream_out, input_out, qkv_g, out_g, up_g, down_g, qkv_a, out_a, up_a, down_a, qkv_b, out_b, up_b, down_b,
    qkvrows, qkvcols, outrows, outcols, uprows, upcols, downrows, downcols,
    vec_g, bias_g, vec_m, bias_m, vec_a, bias_a, update_scale, token_spread, held, sems,
):
    f32 = jnp.float32
    groups, rows, width = reduced.shape
    load = pltpu.make_async_copy(stream_in, held, sems.at[0])
    load.start()
    span = input_in.shape[2]
    for i in range(n_mp):
        input_out[:, i * span : (i + 1) * span] = input_in[i].astype(f32)
    load.wait()
    store = pltpu.make_async_copy(held, stream_out, sems.at[1])
    store.start()
    whole = float(rows * n_dp)
    entries = (3.0 * whole * whole, whole * whole, 4.0 * whole * whole, 4.0 * whole * whole)
    row1 = lax.broadcasted_iota(jnp.int32, (8, 1), 0)
    size = jnp.where(row1 == 0, entries[0], jnp.where(row1 == 1, entries[1], entries[2]))
    copies = jnp.where((row1 == SUB_QKV) | (row1 == SUB_UP), float(n_mp), float(n_dp))
    length = jnp.where(row1 == SUB_DOWN, 4.0 * whole, whole)
    mean_rows = DECAY * scalars[:, 3:4] / (copies * length) + (1.0 - DECAY) * (scalars[:, 2:3] / size + square_eps)
    scale = jnp.sqrt(scalars[:, 0:1] * mean_rows / size)
    rms = jnp.sqrt(scalars[:, 1:2] / size)
    rate = step_rate * rms / jnp.maximum(1.0, scale / clip_limit)
    sub = lax.dot_general(
        jnp.where(
            lax.broadcasted_iota(jnp.int32, (rows, LANES), 0) == lax.broadcasted_iota(jnp.int32, (rows, LANES), 1), 1.0, 0.0
        ),
        sub_new[...], NT, precision=EXACT, preferred_element_type=f32,
    )
    is_o = o_lanes(width)

    def renewed(group, index):
        gradient = reduced[group]
        product = sub[:, index : index + 1] * lane_new[group : group + 1] / mean_rows[index : index + 1]
        return masters[group] - rate[index : index + 1] * (gradient * lax.rsqrt(product))

    def spread(value, qkv, out):
        q, k, v, o = unpack_lanes(value)
        for i, part in enumerate((q, k, v)):
            qkv[i] = part.astype(qkv.dtype)
        out[...] = o.T.astype(out.dtype)

    first = jnp.where(is_o > 0.0, renewed(2, 1), renewed(2, 0))
    spread(reduced[2], qkv_g, out_g)
    spread(first, qkv_a, out_a)
    spread(first, qkv_b, out_b)
    for group, index, grad, after, short in ((0, 2, up_g, up_a, up_b), (1, 3, down_g, down_a, down_b)):
        new = renewed(group, index)
        grad[...] = reduced[group]
        after[...] = new
        short[...] = new.astype(short.dtype)

    def plain(weight, gradient, moment_old, together):
        moment = DECAY * moment_old + (1.0 - DECAY) * (gradient * gradient + square_eps)
        update = gradient * lax.rsqrt(moment)
        update_mean = jnp.mean(update * update, axis=1, keepdims=True)
        weight_mean = jnp.mean(weight * weight, axis=1, keepdims=True)
        if together is not None:
            row = lax.broadcasted_iota(jnp.int32, update_mean.shape, 0)
            number = float(weight.shape[0] - together)

            def join(mean):
                shared = jnp.sum(jnp.where(row >= together, mean, 0.0), axis=0, keepdims=True) / number
                return jnp.where(row >= together, shared, mean)

            update_mean, weight_mean = join(update_mean), join(weight_mean)
        rate_here = step_rate * jnp.sqrt(weight_mean)
        return weight - rate_here * update / jnp.maximum(1.0, jnp.sqrt(update_mean) / clip_limit), moment

    vec_g[...] = sums[0:8]
    bias_g[...] = sums[8:14]
    vec_a[...], vec_m[...] = plain(vec[...], sums[0:8], vec_moment[...], None)
    bias_a[...], bias_m[...] = plain(bias[...], sums[8:14], bias_moment[...], 2)
    spreads = jnp.sqrt(sums[14:15, 0:LANES] / (sums[14:15, 3:4] * width))
    scales = jnp.zeros((1, LANES), f32)
    lane1 = lax.broadcasted_iota(jnp.int32, (1, LANES), 1)
    for i in range(4):
        scales = scales + jnp.where(lane1 == i, scale[i : i + 1], 0.0)
    update_scale[...] = scales[:, 0:4].reshape(4)
    token_spread[...] = spreads[:, 0:3].reshape(3)
    for index, ref in ((SUB_QKV, qkvrows), (SUB_OUT, outcols), (SUB_UP, uprows), (SUB_DOWN, downcols)):
        ref[...] = sub_new[index, 0:rows]
    upcols[...] = lane_new[0]
    downrows[...] = lane_new[1]
    *cols, out_row = unpack_lanes(lane_new[2:3])
    for i in range(3):
        qkvcols[i : i + 1] = cols[i]
    outrows[...] = out_row.reshape(out_row.shape[1])
    store.wait()


def bias_rows_natural(qkv_sums, hidden_sums, n_mp, width):
    f32 = jnp.float32
    share = width // n_mp
    half = LANES // 2
    query = [qkv_sums[m : m + 1, a:b] for m in range(n_mp) for a, b in ((0, LANES), (512, 512 + half))]
    value = [qkv_sums[m : m + 1, a:b] for m in range(n_mp) for a, b in ((256, 256 + LANES), (704, 704 + half))]
    source = lax.broadcasted_iota(jnp.int32, (width, width), 0)
    target = lax.broadcasted_iota(jnp.int32, (1, width), 1)
    fan = width // share
    from_lane = target * fan
    for r in range(1, fan):
        from_lane = jnp.where(target >= r * share, (target - r * share) * fan + r, from_lane)
    move = jnp.where(source == from_lane, 1.0, 0.0).astype(jnp.bfloat16)
    moved = jnp.zeros_like(hidden_sums)
    left = hidden_sums
    for _ in range(3):
        part = left.astype(jnp.bfloat16)
        moved = moved + mm(part, move)
        left = left - part.astype(f32)
    rows = [jnp.concatenate(query, axis=1), jnp.concatenate(value, axis=1)]
    for r in range(width // share):
        rows.append(
            jnp.concatenate([moved[m : m + 1, r * share : (r + 1) * share] for m in range(n_mp)], axis=1)
        )
    return rows

class Stream:
    CUTS = 4

    def __init__(self, n_mp, src, out, send_sems, recv_sems):
        self.dp, self.mp, self.n_mp = lax.axis_index("dp"), lax.axis_index("mp"), n_mp
        self.src, self.out, self.send_sems, self.recv_sems = src, out, send_sems, recv_sems
        self.rows = out.shape[1] // self.CUTS
        self.up, self.down = jnp.minimum(self.mp + 1, n_mp - 1), jnp.maximum(self.mp - 1, 0)

    def message(self, plane, cut, way, own):
        part = pl.ds(pl.multiple_of(cut * self.rows, self.rows), self.rows)
        where = self.out.at[plane, part]
        return pltpu.make_async_remote_copy(
            src_ref=self.src.at[part] if own else where,
            dst_ref=where,
            send_sem=self.send_sems.at[way, plane, cut],
            recv_sem=self.recv_sems.at[plane, cut],
            device_id=(self.dp, self.down if way else self.up),
            device_id_type=MESH,
        )

    def step(self, s):
        distance, cut = s // self.CUTS, s % self.CUTS
        mp, last = self.mp, self.n_mp - 1

        @pl.when((distance == 0) & (mp < last))
        def _():
            self.message(mp, cut, 0, True).start()

        @pl.when((distance == 0) & (mp > 0))
        def _():
            self.message(mp, cut, 1, True).start()

        below, above = mp - distance, mp + distance

        @pl.when((distance > 0) & (below >= 0))
        def _():
            self.message(below, cut, 0, False).wait_recv()

            @pl.when(mp < last)
            def _():
                self.message(below, cut, 0, False).start()

        @pl.when((distance > 0) & (above <= last))
        def _():
            self.message(above, cut, 1, False).wait_recv()

            @pl.when(mp > 0)
            def _():
                self.message(above, cut, 1, False).start()

    STEPS = 16

    def finish(self):
        mp, last = self.mp, self.n_mp - 1

        def body(t, _):
            plane, cut = t // self.CUTS, t % self.CUTS

            @pl.when((plane <= mp) & (mp < last))
            def _():
                self.message(plane, cut, 0, False).wait_send()

            @pl.when((plane >= mp) & (mp > 0))
            def _():
                self.message(plane, cut, 1, False).wait_send()

            return 0

        lax.fori_loop(0, self.n_mp * self.CUTS, body, 0)

def layer_kernel(
    n_dp, n_mp, slots, own_rows, tokens_in, cot_in, w_qkv, w_out, w_up, w_down_t, counts, vec, biases, *rest
):
    (
        qkvrows, qkvcols, outrows, outcols, uprows, upcols, downrows, downcols,
        masters, reduced, sums_out, sub_out, lane_out, scalar_out, input_out, stream_out,
        w, tokens, cot, qkv, active, slope, mixed, proj, normed_two, normed_t, normed_two_t, turned_t, branch, d_branch, d_two,
        result, feat_q, feat_k, d_mixed, acc, d_query, bias, sums, sums_qkv, sub_prior, lane_prior,
        pair_in, halves_in, x_in, y_in, z_in, value, swap_in, early_mp, early_dp, late_mp, late_dp, last_mp, last_dp,
        credit, local_sems, g_send, g_recv, g_way, s_send, s_recv, stream_send, stream_recv, turn_send, turn_recv,
        swap_send, swap_recv, small_send, small_recv,
    ) = rest
    set_rows, width = tokens.shape
    place = Place(set_rows, own_rows)
    window, own, own_start, window_start, tiles = (
        place.window, place.own, place.own_start, place.window_start, place.tiles
    )
    low, f32 = jnp.bfloat16, jnp.float32
    dp, mp = lax.axis_index("dp"), lax.axis_index("mp")
    in_set = pl.ds(pl.multiple_of(place.set_index * set_rows, LANES), set_rows)
    token_copy = pltpu.make_async_copy(tokens_in.at[in_set], tokens, local_sems.at[0])
    in_window = pl.ds(pl.multiple_of(place.set_index * set_rows + window_start, LANES), window)
    cot_copy = pltpu.make_async_copy(cot_in.at[in_window], cot, local_sems.at[1])
    token_copy.start()
    cot_copy.start()
    net = Gather(n_mp, w, g_send, g_recv, g_way)
    back = Scatter(n_mp, w, reduced, (pair_in, halves_in, x_in, y_in, z_in), credit, s_send, s_recv)
    stream = Stream(n_mp, result, stream_out, stream_send, stream_recv)
    swaps = Doubling(value, swap_in, swap_send, swap_recv)
    exchanges = [
        Exchange(axis, size, buf, small_send.at[i], small_recv.at[i])
        for i, (axis, size, buf) in enumerate(
            (
                ("mp", n_mp, early_mp), ("dp", n_dp, early_dp), ("mp", n_mp, late_mp), ("dp", n_dp, late_dp),
                ("mp", n_mp, last_mp), ("dp", n_dp, last_dp),
            )
        )
    ]
    masters[0] = w_up[...]
    masters[1] = w_down_t[...]
    pack_first(w_qkv, w_out, masters.at[2])
    for group, source in enumerate((2, 0, 1)):
        w[group, mp, dp // 2, dp % 2] = masters[source].astype(low)
    greet(
        [((dp + away) % n_dp, mp) for away in range(1, n_dp)] + [(dp, (mp + away) % n_mp) for away in range(1, n_mp)], []
    )
    net.begin()

    def weight(group, m, lanes=None):
        block = w[group, m] if lanes is None else w[group, m, :, :, :, lanes]
        return block.reshape(width, block.shape[-1])

    pack_biases(biases, bias, n_mp, width)
    total = make_features(counts, place.set_index, slots, set_rows, feat_q, feat_k)
    token_copy.wait()
    zero_row = jnp.zeros((1, width), f32)
    normed = slope

    def norm_one(i, _):
        unit, _inv = row_stats(tokens[tile_rows(i)].astype(f32))
        per_half = own_rows // LANES
        normed[i // per_half, tile_rows(i % per_half)] = (unit * vec[0:1] + vec[1:2]).astype(low)
        return 0

    lax.fori_loop(0, set_rows // LANES, norm_one, 0)
    net.step(0)
    cot_copy.wait()

    def back_of(i):
        return cot[tile_rows(i)].astype(f32) * place.valid(i, total)

    def first_grad(i, total_row):
        db = (back_of(i) * vec[5:6]).astype(low)
        d_branch[tile_rows(i)] = db
        return total_row + place.is_own(i) * column_sum(db.astype(f32))

    branch_sum = lax.fori_loop(0, tiles, first_grad, zero_row)
    turned_t[...] = d_branch[own].T
    net.step(1)
    normed_t[...] = normed[mp % 2, 0:own_rows].T

    def project(u, _):
        net.step(u + 2)
        net.stage_d(u)
        m = net.plane(u)
        for half in range(set_rows // own_rows):
            at = pl.ds(half * own_rows, own_rows)
            qkv[m, at] = (mm(normed[half, 0:own_rows], weight(0, m)) + bias[pl.ds(m, 1)]).astype(low)
        attend(m, qkv, mixed, feat_q, feat_k, window_start, window, window // 2)
        return 0

    project(0, 0)
    lax.fori_loop(1, n_mp, project, 0)
    net.step(n_mp + 2)
    proj[...] = sum((mm(mixed[m], weight(0, m, pl.ds(MIX, 2 * LANES)), NT) for m in range(n_mp)), vec[6:7])

    def middle_of(i):
        return tokens[tile_rows(i, window_start)].astype(f32) + vec[4:5] * proj[tile_rows(i)]

    def norm_two(i, _):
        unit, _inv = row_stats(middle_of(i))
        normed_two[tile_rows(i)] = (unit * vec[2:3] + vec[3:4]).astype(low)
        return 0

    lax.fori_loop(0, tiles, norm_two, 0)
    normed_two_t[...] = normed_two[own].T

    half_shape = (n_dp // 2, 2, width // n_dp)

    def keep(group, m, lanes, block):
        w[group, m, :, :, :, lanes] = block.astype(low).reshape(*half_shape, block.shape[1])

    def feed(u, _):
        first_unit = n_mp + 2 * u
        net.stage_d(first_unit)
        net.stage_d(first_unit + 1)
        m = net.plane(u)

        def rows(i, _):
            at = tile_rows(i)
            hidden = mm(normed_two[at], weight(1, m)) + bias[pl.ds(n_mp + m, 1)]
            act, slp = gelu_parts(hidden)
            slope[m, at] = slp.astype(low)

            @pl.when((i * LANES >= own_start) & (i * LANES < own_start + own_rows))
            def _():
                active[m, tile_rows(i - own_start // LANES)] = act.astype(low)

            return 0

        lax.fori_loop(0, tiles, rows, 0)
        net.step(first_unit + 3)
        part_sum = mm(active[m], weight(2, m), NT)

        @pl.when(u == 0)
        def _():
            branch[...] = part_sum

        @pl.when(u > 0)
        def _():
            branch[...] += part_sum

        def grad_rows(i, total_row):
            at = tile_rows(i)
            dh = (mm(d_branch[at], weight(2, m)) * slope[m, at].astype(f32)).astype(low)
            slope[m, at] = dh
            return total_row + place.is_own(i) * column_sum(dh.astype(f32))

        sums[pl.ds(8 + m, 1)] = lax.fori_loop(0, tiles, grad_rows, zero_row)
        net.step(first_unit + 4)
        two_sum = mm(slope[m], weight(1, m), NT)

        @pl.when(u == 0)
        def _():
            d_two[...] = two_sum

        @pl.when(u > 0)
        def _():
            d_two[...] += two_sum

        @pl.when(u > 0)
        def _():
            for o in (2 * u - 2, 2 * u - 1):
                back.add_pair(o, *back.offered(o))

        net.finish(first_unit)
        net.finish(first_unit + 1)
        everything = pl.ds(0, width)
        keep(2, m, everything, mm(turned_t[...], active[m]))
        back.offer(2 * u, 2, m)
        keep(1, m, everything, mm(normed_two_t[...], slope[m, own]))
        back.offer(2 * u + 1, 1, m)
        return 0

    lax.fori_loop(0, n_mp, feed, 0)

    def final(i, carry):
        there = own_start // LANES + i
        br = branch[tile_rows(i)] + vec[7:8]
        scaled = vec[5:6] * br
        res = middle_of(there) + scaled
        result[tile_rows(i)] = res.astype(low)
        attn = vec[4:5] * proj[tile_rows(there)]
        valid = place.valid(there, total)
        new = [column_sum(valid * v * v) for v in (res, attn, scaled)] + [column_sum(back_of(there) * br)]
        return tuple(c + n for c, n in zip(carry, new))

    *squares, back_branch = lax.fori_loop(0, own_rows // LANES, final, (zero_row,) * 4)
    own_result = pltpu.make_async_copy(result, stream_out.at[mp], local_sems.at[2])
    own_result.start()
    for cut in range(stream.CUTS):
        stream.step(cut)
    fed = 2 * n_mp
    for o in (fed - 2, fed - 1):
        back.add_pair(o, *back.offered(o))

    d_proj, d_proj_t = d_branch, turned_t

    def norm_two_back(i, carry):
        at = tile_rows(i)
        grad = d_two[at]
        dv, grad_unit = norm_grad(middle_of(i), vec[2:3], grad)
        d_mid = back_of(i) + dv
        d_two[at] = d_mid
        d_out = (d_mid * vec[4:5]).astype(low)
        d_proj[at] = d_out
        mine = place.is_own(i)
        new = (grad_unit, grad, d_mid * proj[at], d_out.astype(f32))
        return tuple(c + mine * column_sum(n) for c, n in zip(carry, new))

    gain_two, shift_two, scale_sum, proj_sum = lax.fori_loop(0, tiles, norm_two_back, (zero_row,) * 4)
    d_proj_t[...] = d_proj[own].T
    for u in range(n_mp):
        net.finish(u)
    d_normed = branch
    d_qkv = normed_two.at[pl.ds(0, own_rows)]

    def slot(k):
        back.slot(k)
        stream.step(k + stream.CUTS)

    def attention(u, _):
        m = plane_at(mp, n_mp - 1 - u)

        @pl.when(u > 0)
        def _():
            back.add_pair(fed + u - 1, 0, plane_at(mp, n_mp - u))

        dm = mm(d_proj[...], weight(0, m, pl.ds(MIX, 2 * LANES))).astype(low)
        d_mixed[:, 0:LANES] = dm[:, 0:LANES]
        d_mixed[:, LANES:] = keep_half(1, dm[:, LANES:], jnp.zeros_like(dm[:, LANES:]))
        slot(2 * u)
        attend_back(m, qkv, d_mixed, feat_q, feat_k, window_start, window, acc, d_query)
        slot(2 * u + 1)
        d_qkv[:, 0:128] = d_query[own, 0:128]
        d_qkv[:, 128:256] = acc[own, 0:128].astype(low)
        d_qkv[:, 256:384] = acc[own, 128:256].astype(low)
        d_qkv[:, 384:512] = jnp.zeros((own_rows, LANES), low)
        d_qkv[:, 512:640] = d_query[own, 128:256]
        d_qkv[:, 640:768] = acc[own, 256:384].astype(low)
        sums_qkv[pl.ds(m, 1)] = column_sum(d_qkv[...].astype(f32))
        part_sum = mm(d_qkv[...], weight(0, m), NT)

        @pl.when(u == 0)
        def _():
            d_normed[...] = part_sum

        @pl.when(u > 0)
        def _():
            d_normed[...] += part_sum

        block = mm(normed_t[...], d_qkv[...])
        extra = mm(d_proj_t[...], mixed[m, own])
        keep(0, m, pl.ds(0, MIX), block[:, 0:MIX])
        keep(0, m, pl.ds(MIX, 2 * LANES), block[:, MIX : MIX + 2 * LANES] + extra)
        keep(0, m, pl.ds(MIX + 2 * LANES, LANES), block[:, MIX + 2 * LANES :])
        back.offer(fed + u, 0, m)
        return 0

    lax.fori_loop(0, n_mp, attention, 0)
    slot(fed)
    back.add_pair(back.units - 1, 0, mp)

    input_t = normed_t

    def norm_one_back(i, carry):
        grad = d_normed[tile_rows(i)]
        rows = tokens[tile_rows(own_start // LANES + i, window_start)].astype(f32)
        dv, grad_unit = norm_grad(rows, vec[0:1], grad)
        input_t[:, tile_rows(i)] = (d_two[tile_rows(i, own_start)] + dv).astype(low).T
        return tuple(c + column_sum(n) for c, n in zip(carry, (grad_unit, grad)))

    gain_one, shift_one = lax.fori_loop(0, own_rows // LANES, norm_one_back, (zero_row, zero_row))
    share = width // n_mp

    def turn(away):
        peer = (mp + away) % n_mp
        return pltpu.make_async_remote_copy(
            src_ref=input_t.at[pl.ds(pl.multiple_of(peer * share, HD), share)],
            dst_ref=input_out.at[mp],
            send_sem=turn_send.at[away],
            recv_sem=turn_recv.at[away],
            device_id={"mp": peer},
            device_id_type=MESH,
        )

    def turned(away):
        source = (mp - away + n_mp) % n_mp
        return pltpu.make_async_remote_copy(
            src_ref=input_t.at[pl.ds(0, share)],
            dst_ref=input_out.at[source],
            send_sem=turn_send.at[away],
            recv_sem=turn_recv.at[away],
            device_id={"mp": source},
            device_id_type=MESH,
        )

    for away in range(1, n_mp):
        turn(away).start()
    own_turn = pltpu.make_async_copy(
        input_t.at[pl.ds(pl.multiple_of(mp * share, HD), share)], input_out.at[mp], local_sems.at[3]
    )
    own_turn.start()
    slot(fed + 1)

    held = jnp.clip(total - (window_start + own_start), 0, own_rows).astype(f32)
    lane_w = lax.broadcasted_iota(jnp.int32, (1, width), 1)
    scalar_row = jnp.where(lane_w == 3, held, 0.0)
    for i in range(3):
        scalar_row = scalar_row + jnp.where(lane_w == i, jnp.sum(squares[i], axis=1, keepdims=True), 0.0)
    natural = bias_rows_natural(sums_qkv[0:n_mp], sums[8 : 8 + n_mp], n_mp, width)
    vector_rows = [gain_one, shift_one, gain_two, shift_two, scale_sum, back_branch, proj_sum, branch_sum]
    for i, row in enumerate(vector_rows + natural + [scalar_row, zero_row]):
        value[0, i : i + 1] = row
    swaps.send(0)
    rows_here = qkvrows.shape[0]
    sub_prior[...] = jnp.zeros_like(sub_prior)
    for i, prior in enumerate((qkvrows, outcols, uprows, downcols)):
        sub_prior[i : i + 1, 0:rows_here] = prior[...][None, :]
    lane_prior[0:1] = upcols[...][None, :]
    lane_prior[1:2] = downrows[...][None, :]
    lane_prior[2:3] = pack_lanes([qkvcols[i : i + 1] for i in range(3)], outrows[...][None, :])
    sub_out[...] = jnp.zeros_like(sub_out)
    lane_out[...] = jnp.zeros_like(lane_out)
    factors = Factors(reduced, sub_prior, lane_prior, n_dp, exchanges)
    early, late = (0, 1), (2,)
    slot(fed + 2)
    swaps.add(0)
    swaps.send(1)
    factors.send(early, factors.early_mp, factors.early_dp)
    slot(fed + 3)
    swaps.add(1)
    swaps.send(2)
    slot(fed + 4)
    swaps.add(2)
    swaps.send(3)
    factors.collect(early, factors.early_mp, factors.early_dp, sub_out, lane_out)
    slot(fed + 5)
    factors.send(late, factors.late_mp, factors.late_dp)
    swaps.add(3)
    swaps.send(4)
    factors.collect(late, factors.late_mp, factors.late_dp, sub_out, lane_out)
    factors.finish(masters, scalar_out)
    swaps.add(4)
    sums_out[...] = value[5]
    for s in range(fed + 5 + stream.CUTS + 1, stream.STEPS):
        stream.step(s)
    for away in range(1, n_mp):
        turned(away).wait_recv()
        turn(away).wait_send()
    own_turn.wait()
    own_result.wait()
    factors.wait_sends()
    back.finish()
    stream.finish()
    swaps.finish()

def moments_of(stream):
    center = stream - jnp.mean(stream, axis=-1, keepdims=True)
    spread = jnp.mean(center * center, axis=-1, keepdims=True)
    return (center, lax.rsqrt(spread + norm_eps))


def normalize(stream, gain_row, shift_row):
    center, inverse = moments_of(stream)
    return center * inverse * gain_row + shift_row


def segment_ids(counts, set_rows):
    image_ends = jnp.cumsum(counts)
    places = jnp.arange(set_rows, dtype=jnp.int32)
    return jnp.sum((places[:, None] >= image_ends[None, :]).astype(jnp.int32), axis=1)


def scores_of(query_set, key_set, same_image, score_scale):
    raw_scores = (
        jnp.einsum("qhd,khd->hqk", query_set, key_set, preferred_element_type=jnp.float32)
        * score_scale
    )
    return jnp.where(same_image[None], raw_scores, mask_fill)


def shard_offset(shard_piece, block_index, whole_length, axis_at):
    shape_list = list(shard_piece.shape)
    shape_list[axis_at] = whole_length
    empty = jnp.zeros(tuple(shape_list), jnp.float32)
    return lax.dynamic_update_slice_in_dim(
        empty, shard_piece, block_index * shard_piece.shape[axis_at], axis_at
    )


def select_slice(whole_array, block_index, block_width, axis_at):
    return lax.dynamic_slice_in_dim(whole_array, block_index * block_width, block_width, axis_at)


def factor_step(
    gradient,
    rows_old,
    cols_old,
    rows_mine,
    cols_mine,
    rows_total,
    count_rows,
    count_cols,
    prior_total,
):
    decay_rate = 1.0 - STEP ** (-0.8)
    rows_new = decay_rate * rows_old + (1.0 - decay_rate) * (rows_mine / count_cols + square_eps)
    cols_new = decay_rate * cols_old + (1.0 - decay_rate) * (cols_mine / count_rows + square_eps)
    rows_average = (
        decay_rate * prior_total
        + (1.0 - decay_rate) * (rows_total / count_cols + count_rows * square_eps)
    ) / count_rows
    update = gradient * lax.rsqrt(rows_new[:, None] * cols_new[None, :] / rows_average)
    return (rows_new, cols_new, update, jnp.sum(update * update))


def plain_step(weight, gradient, moment_old):
    decay_rate = 1.0 - STEP ** (-0.8)
    moment = decay_rate * moment_old + (1.0 - decay_rate) * (gradient * gradient + square_eps)
    update = gradient * lax.rsqrt(moment)
    update_rms = jnp.sqrt(jnp.mean(update * update))
    rate_here = step_rate * jnp.sqrt(jnp.mean(weight * weight))
    return (weight - rate_here * update / jnp.maximum(1.0, update_rms / clip_limit), moment)


def generic(
    tokens_in,
    cotangent,
    patch_counts,
    w_qkv,
    w_out,
    w_up,
    w_down,
    layer_vector_rows,
    inner_biases,
    qkvrows_prior,
    qkvcols_prior,
    outrows_prior,
    outcols_prior,
    uprows_prior,
    upcols_prior,
    downrows_prior,
    downcols_prior,
    vector_moment,
    bias_moment,
):
    data_index = lax.axis_index("dp")
    parallel_model_index = lax.axis_index("mp")
    row_count, parallel_model_width = tokens_in.shape
    set_count, slot_count = patch_counts.shape
    set_rows = row_count // set_count
    shard_width_local = w_qkv.shape[2]
    local_hidden = w_up.shape[1]
    head_count = shard_width_local // HD
    score_scale = HD ** (-0.5)
    full_qkv, full_out, full_up, full_down = (
        lax.all_gather(w_qkv.astype(jnp.bfloat16), "dp", axis=0, tiled=True),
        lax.all_gather(w_out.astype(jnp.bfloat16), "dp", axis=1, tiled=True),
        lax.all_gather(w_up.astype(jnp.bfloat16), "dp", axis=0, tiled=True),
        lax.all_gather(w_down.astype(jnp.bfloat16), "dp", axis=1, tiled=True),
    )
    stream = tokens_in.astype(jnp.float32)
    segment = jax.vmap(lambda counts: segment_ids(counts, set_rows))(patch_counts)
    valid_rows = (segment < slot_count).astype(jnp.float32).reshape(row_count)
    centered_single, inverse_deviation_single = moments_of(stream)
    standardized_single = centered_single * inverse_deviation_single
    normalized_rows = (standardized_single * layer_vector_rows[0] + layer_vector_rows[1]).astype(
        jnp.bfloat16
    )
    bias_mine = select_slice(inner_biases, parallel_model_index, shard_width_local, 1)
    projected = jnp.einsum(
        "rd,dtc->rtc", normalized_rows, full_qkv, preferred_element_type=jnp.float32
    )
    query_rows = (projected[:, 0] + bias_mine[0]).astype(jnp.bfloat16)
    key_rows = projected[:, 1].astype(jnp.bfloat16)
    value_rows = (projected[:, 2] + bias_mine[1]).astype(jnp.bfloat16)

    def split_sets(field_in):
        return field_in.reshape(set_count, set_rows, head_count, HD)

    def attend(set_item):
        query_set, key_set, value_set, segment_set = set_item
        same_image = segment_set[:, None] == segment_set[None, :]
        raw_scores = scores_of(query_set, key_set, same_image, score_scale)
        row_top = jnp.max(raw_scores, axis=-1, keepdims=True)
        exponent = jnp.exp(raw_scores - row_top)
        row_total = jnp.sum(exponent, axis=-1, keepdims=True)
        weights = exponent / row_total
        mixed_set = jnp.einsum(
            "hqk,khd->qhd",
            weights.astype(jnp.bfloat16),
            value_set,
            preferred_element_type=jnp.float32,
        )
        return (mixed_set.astype(jnp.bfloat16), (row_top + jnp.log(row_total))[..., 0])

    mixed_heads, log_total = lax.map(
        attend, (split_sets(query_rows), split_sets(key_rows), split_sets(value_rows), segment)
    )
    mixed_heads = mixed_heads.reshape(row_count, shard_width_local)
    attn_terms = jnp.dot(mixed_heads, full_out, preferred_element_type=jnp.float32)
    proj = (
        lax.psum(attn_terms.astype(jnp.bfloat16), "mp").astype(jnp.float32) + layer_vector_rows[6]
    )
    shared_mask = shard_offset(
        jnp.ones((shard_width_local,), jnp.float32), parallel_model_index, parallel_model_width, 0
    )
    middle = stream + layer_vector_rows[4] * proj
    normed_here = normalize(middle, layer_vector_rows[2], layer_vector_rows[3]).astype(jnp.bfloat16)
    up_bias = select_slice(inner_biases[2:], parallel_model_index, shard_width_local, 1).T.reshape(
        local_hidden
    )
    hidden = jnp.dot(normed_here, full_up, preferred_element_type=jnp.float32) + up_bias
    active = jax.nn.gelu(hidden, approximate=False).astype(jnp.bfloat16)
    mlp_terms = jnp.dot(active, full_down, preferred_element_type=jnp.float32)
    branch = (
        lax.psum(mlp_terms.astype(jnp.bfloat16), "mp").astype(jnp.float32) + layer_vector_rows[7]
    )
    result = middle + layer_vector_rows[5] * branch
    result_low = result.astype(jnp.bfloat16)
    back_grad = cotangent.astype(jnp.float32) * valid_rows[:, None]
    d_branch = (back_grad * layer_vector_rows[5]).astype(jnp.bfloat16)
    down_part = jnp.einsum("rf,rd->fd", active, d_branch, preferred_element_type=jnp.float32)
    d_active = jnp.einsum("rd,fd->rf", d_branch, full_down, preferred_element_type=jnp.float32)
    gelu_out, gelu_pull = jax.vjp(lambda inputs: jax.nn.gelu(inputs, approximate=False), hidden)
    d_hidden = gelu_pull(d_active)[0].astype(jnp.bfloat16)
    up_part = jnp.einsum("rd,rf->df", normed_here, d_hidden, preferred_element_type=jnp.float32)
    mid_terms = jnp.einsum("rf,df->rd", d_hidden, full_up, preferred_element_type=jnp.float32)
    d_normed_two = lax.psum(mid_terms.astype(jnp.bfloat16), "mp").astype(jnp.float32)
    norm_out, norm_pull = jax.vjp(normalize, middle, layer_vector_rows[2], layer_vector_rows[3])
    d_through, d_gain_two, d_shift_two = norm_pull(d_normed_two)
    d_middle = back_grad + d_through
    d_proj_here = (d_middle * layer_vector_rows[4]).astype(jnp.bfloat16)
    d_middle_cols = select_slice(d_middle, parallel_model_index, shard_width_local, 1)
    out_part = jnp.einsum("rc,rd->cd", mixed_heads, d_proj_here, preferred_element_type=jnp.float32)
    d_mixed = jnp.einsum(
        "rd,cd->rc", d_proj_here, full_out, preferred_element_type=jnp.float32
    ).astype(jnp.bfloat16)

    def attend_back(set_item):
        query_set, key_set, value_set, segment_set, total_set, grad_set = set_item
        same_image = segment_set[:, None] == segment_set[None, :]
        raw_scores = scores_of(query_set, key_set, same_image, score_scale)
        weights = jnp.exp(raw_scores - total_set[..., None])
        d_value = jnp.einsum(
            "hqk,qhd->khd",
            weights.astype(jnp.bfloat16),
            grad_set,
            preferred_element_type=jnp.float32,
        )
        d_weights = jnp.einsum(
            "qhd,khd->hqk", grad_set, value_set, preferred_element_type=jnp.float32
        )
        d_scores = (
            weights * (d_weights - jnp.sum(d_weights * weights, axis=-1, keepdims=True))
        ).astype(jnp.bfloat16)
        d_query = (
            jnp.einsum("hqk,khd->qhd", d_scores, key_set, preferred_element_type=jnp.float32)
            * score_scale
        )
        d_key = (
            jnp.einsum("hqk,qhd->khd", d_scores, query_set, preferred_element_type=jnp.float32)
            * score_scale
        )
        return jnp.stack([d_query, d_key, d_value], axis=1).astype(jnp.bfloat16)

    d_projected = lax.map(
        attend_back,
        (
            split_sets(query_rows),
            split_sets(key_rows),
            split_sets(value_rows),
            segment,
            log_total,
            split_sets(d_mixed),
        ),
    )
    d_projected = d_projected.reshape(row_count, 3, shard_width_local)
    qkv_part = jnp.einsum(
        "rd,rtc->dtc", normalized_rows, d_projected, preferred_element_type=jnp.float32
    )
    normalized_gradient = lax.psum_scatter(
        jnp.einsum("rtc,dtc->rd", d_projected, full_qkv, preferred_element_type=jnp.float32).astype(
            jnp.bfloat16
        ),
        "mp",
        scatter_dimension=1,
        tiled=True,
    ).astype(jnp.float32)
    standardized_local = select_slice(
        standardized_single, parallel_model_index, shard_width_local, 1
    )
    local_gain_slice = select_slice(
        layer_vector_rows[0], parallel_model_index, shard_width_local, 0
    )
    standardized_gradient = normalized_gradient * local_gain_slice
    gradient_sum_local, product_sum_local = lax.psum(
        (
            jnp.sum(standardized_gradient, axis=1),
            jnp.sum(standardized_gradient * standardized_local, axis=1),
        ),
        "mp",
    )
    input_grad = d_middle_cols + inverse_deviation_single * (
        standardized_gradient
        - gradient_sum_local[:, None] / parallel_model_width
        - standardized_local * product_sum_local[:, None] / parallel_model_width
    )

    def mine(field_in):
        return select_slice(field_in, parallel_model_index, shard_width_local, field_in.ndim - 1)

    vector_part = jnp.stack(
        [
            shard_offset(
                jnp.sum(normalized_gradient * standardized_local, axis=0),
                parallel_model_index,
                parallel_model_width,
                0,
            ),
            shard_offset(
                jnp.sum(normalized_gradient, axis=0), parallel_model_index, parallel_model_width, 0
            ),
            d_gain_two * shared_mask,
            d_shift_two * shared_mask,
            jnp.sum(d_middle * proj, axis=0) * shared_mask,
            jnp.sum(back_grad * branch, axis=0) * shared_mask,
            shard_offset(
                jnp.sum(mine(d_proj_here).astype(jnp.float32), axis=0),
                parallel_model_index,
                parallel_model_width,
                0,
            ),
            shard_offset(
                jnp.sum(mine(d_branch).astype(jnp.float32), axis=0),
                parallel_model_index,
                parallel_model_width,
                0,
            ),
        ]
    )
    hidden_sums = (
        jnp.sum(d_hidden.astype(jnp.float32), axis=0)
        .reshape(shard_width_local, local_hidden // shard_width_local)
        .T
    )
    bias_part = jnp.concatenate(
        [
            jnp.sum(d_projected[:, 0].astype(jnp.float32), axis=0)[None],
            jnp.sum(d_projected[:, 2].astype(jnp.float32), axis=0)[None],
            hidden_sums,
        ],
        axis=0,
    )
    squares = jnp.stack(
        [
            jnp.sum(valid_rows[:, None] * shared_mask * field_in * field_in)
            for field_in in (result, layer_vector_rows[4] * proj, layer_vector_rows[5] * branch)
        ]
    )
    counted = jnp.where(parallel_model_index == 0, jnp.sum(valid_rows), 0.0)
    vector_grad, bias_grad, squares_all, counted_all = lax.psum(
        (
            vector_part,
            shard_offset(bias_part, parallel_model_index, parallel_model_width, 1),
            squares,
            counted,
        ),
        ("dp", "mp"),
    )
    token_spread = jnp.sqrt(squares_all / (counted_all * parallel_model_width))
    grad_parts = (qkv_part, out_part, up_part, down_part)
    summed = lax.psum((grad_parts[0], grad_parts[1], grad_parts[2], grad_parts[3]), "dp")
    qkv_grad = select_slice(summed[0], data_index, w_qkv.shape[0], 0)
    out_grad = select_slice(summed[1], data_index, w_out.shape[1], 1)
    up_grad = select_slice(summed[2], data_index, w_up.shape[0], 0)
    down_grad = select_slice(summed[3], data_index, w_down.shape[1], 1)
    square_qkv = qkv_grad * qkv_grad
    square_out = out_grad * out_grad
    square_up = up_grad * up_grad
    square_down = down_grad * down_grad
    scalars = jnp.stack(
        [
            jnp.sum(w_qkv * w_qkv),
            jnp.sum(w_out * w_out),
            jnp.sum(w_up * w_up),
            jnp.sum(w_down * w_down),
            jnp.where(parallel_model_index == 0, jnp.sum(qkvrows_prior), 0.0),
            jnp.where(data_index == 0, jnp.sum(outrows_prior), 0.0),
            jnp.where(parallel_model_index == 0, jnp.sum(uprows_prior), 0.0),
            jnp.where(data_index == 0, jnp.sum(downrows_prior), 0.0),
        ]
    )
    factor_totals = lax.psum(
        (
            shard_offset(jnp.sum(square_qkv, axis=(1, 2)), data_index, parallel_model_width, 0),
            shard_offset(
                jnp.sum(square_qkv, axis=0), parallel_model_index, parallel_model_width, 1
            ),
            shard_offset(
                jnp.sum(square_out, axis=1), parallel_model_index, parallel_model_width, 0
            ),
            shard_offset(jnp.sum(square_out, axis=0), data_index, parallel_model_width, 0),
            shard_offset(jnp.sum(square_up, axis=1), data_index, parallel_model_width, 0),
            shard_offset(jnp.sum(square_up, axis=0), parallel_model_index, FF, 0),
            shard_offset(jnp.sum(square_down, axis=1), parallel_model_index, FF, 0),
            shard_offset(jnp.sum(square_down, axis=0), data_index, parallel_model_width, 0),
            scalars,
        ),
        ("dp", "mp"),
    )
    (
        rows_qkv,
        cols_qkv,
        rows_out,
        cols_out,
        rows_up,
        cols_up,
        rows_down,
        cols_down,
        scalar_totals,
    ) = factor_totals
    local_rows = w_qkv.shape[0]
    local_cols = w_out.shape[1]
    qkvrows_after, qkvcols_flat, update_qkv, usq_qkv = factor_step(
        qkv_grad.reshape(local_rows, 3 * shard_width_local),
        qkvrows_prior,
        qkvcols_prior.reshape(3 * shard_width_local),
        select_slice(rows_qkv, data_index, local_rows, 0),
        select_slice(cols_qkv, parallel_model_index, shard_width_local, 1).reshape(
            3 * shard_width_local
        ),
        jnp.sum(rows_qkv),
        parallel_model_width,
        3 * parallel_model_width,
        scalar_totals[4],
    )
    outrows_after, outcols_after, update_out, usq_out = factor_step(
        out_grad,
        outrows_prior,
        outcols_prior,
        select_slice(rows_out, parallel_model_index, shard_width_local, 0),
        select_slice(cols_out, data_index, local_cols, 0),
        jnp.sum(rows_out),
        parallel_model_width,
        parallel_model_width,
        scalar_totals[5],
    )
    uprows_after, upcols_after, update_up, usq_up = factor_step(
        up_grad,
        uprows_prior,
        upcols_prior,
        select_slice(rows_up, data_index, local_rows, 0),
        select_slice(cols_up, parallel_model_index, local_hidden, 0),
        jnp.sum(rows_up),
        parallel_model_width,
        FF,
        scalar_totals[6],
    )
    downrows_after, downcols_after, update_down, usq_down = factor_step(
        down_grad,
        downrows_prior,
        downcols_prior,
        select_slice(rows_down, parallel_model_index, local_hidden, 0),
        select_slice(cols_down, data_index, local_cols, 0),
        jnp.sum(rows_down),
        FF,
        parallel_model_width,
        scalar_totals[7],
    )
    usq_totals = lax.psum(jnp.stack([usq_qkv, usq_out, usq_up, usq_down]), ("dp", "mp"))
    entry_counts = jnp.array(
        [
            3.0 * parallel_model_width * parallel_model_width,
            1.0 * parallel_model_width * parallel_model_width,
            1.0 * parallel_model_width * FF,
            1.0 * FF * parallel_model_width,
        ],
        jnp.float32,
    )
    update_scale = jnp.sqrt(usq_totals / entry_counts)
    weight_rms = jnp.sqrt(scalar_totals[:4] / entry_counts)
    limits = jnp.maximum(1.0, update_scale / clip_limit)
    qkv_after = (
        w_qkv.reshape(local_rows, 3 * shard_width_local)
        - step_rate * weight_rms[0] * update_qkv / limits[0]
    ).reshape(w_qkv.shape)
    out_after = w_out - step_rate * weight_rms[1] * update_out / limits[1]
    up_after = w_up - step_rate * weight_rms[2] * update_up / limits[2]
    down_after = w_down - step_rate * weight_rms[3] * update_down / limits[3]
    vectors_after, moment_vectors = jax.vmap(plain_step)(
        layer_vector_rows, vector_grad, vector_moment
    )
    heads_after, heads_moment = jax.vmap(plain_step)(
        inner_biases[:2], bias_grad[:2], bias_moment[:2]
    )
    upper_after, upper_moment = plain_step(
        inner_biases[2:].reshape(FF), bias_grad[2:].reshape(FF), bias_moment[2:].reshape(FF)
    )
    biases_after = jnp.concatenate(
        [heads_after, upper_after.reshape(FF // parallel_model_width, parallel_model_width)], axis=0
    )
    moment_biases = jnp.concatenate(
        [heads_moment, upper_moment.reshape(FF // parallel_model_width, parallel_model_width)],
        axis=0,
    )
    return (
        result_low,
        input_grad,
        qkv_grad,
        out_grad,
        up_grad,
        down_grad,
        qkv_after,
        out_after,
        up_after,
        down_after,
        qkv_after.astype(jnp.bfloat16),
        out_after.astype(jnp.bfloat16),
        up_after.astype(jnp.bfloat16),
        down_after.astype(jnp.bfloat16),
        qkvrows_after,
        qkvcols_flat.reshape(3, shard_width_local),
        outrows_after,
        outcols_after,
        uprows_after,
        upcols_after,
        downrows_after,
        downcols_after,
        vector_grad,
        bias_grad,
        moment_vectors,
        moment_biases,
        vectors_after,
        biases_after,
        update_scale,
        token_spread,
    )

def shards(
    tokens_in,
    cotangent,
    patch_counts,
    w_qkv,
    w_out,
    w_up,
    w_down,
    layer_vector_rows,
    inner_biases,
    qkvrows_prior,
    qkvcols_prior,
    outrows_prior,
    outcols_prior,
    uprows_prior,
    upcols_prior,
    downrows_prior,
    downcols_prior,
    vector_moment,
    bias_moment,
):
    n_dp, n_mp = lax.axis_size("dp"), lax.axis_size("mp")
    row_count, width = tokens_in.shape
    set_count, slot_count = patch_counts.shape
    set_rows = row_count // set_count
    own_rows = row_count // n_mp
    window = own_rows + HALO
    share, hidden_width, block_rows = w_qkv.shape[2], w_up.shape[1], w_up.shape[0]
    f32, low = jnp.float32, jnp.bfloat16
    vmem = pl.BlockSpec(memory_space=pltpu.VMEM)
    anywhere = pl.BlockSpec(memory_space=pl.ANY)
    scalars_in = pl.BlockSpec(memory_space=pltpu.SMEM)
    dma = pltpu.SemaphoreType.DMA
    held = pltpu.VMEM

    def shape(*dims, dtype=low):
        return jax.ShapeDtypeStruct(dims, dtype)

    masters, reduced, sums, sub_new, lane_new, scalar_rows, input_parts, stream = pl.pallas_call(
        functools.partial(layer_kernel, n_dp, n_mp, slot_count, own_rows),
        out_shape=(
            shape(GROUPS, block_rows, width, dtype=f32),
            shape(GROUPS, block_rows, width, dtype=f32),
            shape(16, width, dtype=f32),
            shape(8, LANES, dtype=f32),
            shape(8, width, dtype=f32),
            shape(8, LANES, dtype=f32),
            shape(n_mp, share, own_rows),
            shape(n_mp, own_rows, width),
        ),
        in_specs=[anywhere] * 2 + [vmem] * 4 + [scalars_in] + [vmem] * 10,
        out_specs=(vmem,) * 6 + (anywhere,) * 2,
        scratch_shapes=[
            held((GROUPS, n_mp, n_dp // 2, 2, block_rows, width), low),
            held((set_rows, width), low),
            held((window, width), low),
            held((n_mp, set_rows, width), low),
            held((n_mp, own_rows, hidden_width), low),
            held((n_mp, window, hidden_width), low),
            held((n_mp, window, 2 * LANES), low),
            held((window, width), f32),
            held((window, width), low),
            held((width, own_rows), low),
            held((width, own_rows), low),
            held((width, own_rows), low),
            held((own_rows, width), f32),
            held((window, width), low),
            held((window, width), f32),
            held((own_rows, width), low),
            held((set_rows, LANES), low),
            held((set_rows, LANES), low),
            held((window, 2 * LANES), low),
            held((window, 3 * LANES), f32),
            held((window, 2 * LANES), low),
            held((8, width), f32),
            held((16, width), f32),
            held((8, width), f32),
            held((8, LANES), f32),
            held((3, width), f32),
            held((RING, n_dp // 2, block_rows, width), low),
            held((GROUPS, n_mp, 2, block_rows // 2, width), low),
            held((GROUPS, n_mp, block_rows, width), low),
            held((GROUPS, n_mp, block_rows, width), low),
            held((GROUPS, n_mp + 1, block_rows, width), low),
            held((6, 16, width), f32),
            held((5, 16, width), f32),
            held((n_mp, 8, LANES), f32),
            held((n_dp, 2, width), f32),
            held((n_mp, 8, LANES), f32),
            held((n_dp, 1, width), f32),
            held((n_mp, 8, LANES), f32),
            held((n_dp, 8, LANES), f32),
            pltpu.SemaphoreType.REGULAR,
            dma((4,)),
            dma((GROUPS, n_mp, KINDS)),
            dma((GROUPS, n_mp, KINDS)),
            dma((GROUPS, n_mp, 2)),
            dma((GROUPS, n_mp, R_KINDS)),
            dma((GROUPS, n_mp, R_KINDS)),
            dma((2, n_mp, Stream.CUTS)),
            dma((n_mp, Stream.CUTS)),
            dma((n_mp,)),
            dma((n_mp,)),
            dma((5,)),
            dma((5,)),
            dma((6, max(n_dp, n_mp))),
            dma((6, max(n_dp, n_mp))),
        ],
        compiler_params=pltpu.CompilerParams(
            collective_id=1, has_side_effects=True, vmem_limit_bytes=63 * 2**20
        ),
    )(
        tokens_in, cotangent, w_qkv.transpose(1, 0, 2), w_out, w_up, w_down.T, patch_counts, layer_vector_rows,
        inner_biases, qkvrows_prior, qkvcols_prior, outrows_prior, outcols_prior, uprows_prior, upcols_prior,
        downrows_prior, downcols_prior,
    )

    def both(*dims):
        return (shape(*dims, dtype=f32),) * 2 + (shape(*dims),)

    kinds = [
        both(3, block_rows, share), both(share, block_rows), both(block_rows, width), both(block_rows, width)
    ]
    small = [
        (block_rows,), (3, share), (share,), (block_rows,),
        (block_rows,), (hidden_width,), (hidden_width,), (block_rows,),
    ] + [(8, width), (6, width)] * 3 + [(4,), (3,)]
    outs = pl.pallas_call(
        functools.partial(update_kernel, n_dp, n_mp),
        out_shape=(
            shape(n_mp, own_rows, width),
            shape(share, row_count, dtype=f32),
            *(kind[i] for i in range(3) for kind in kinds),
            *(shape(*dims, dtype=f32) for dims in small),
        ),
        in_specs=[vmem] * 11 + [anywhere],
        out_specs=(anywhere,) + (vmem,) * 29,
        scratch_shapes=[pltpu.VMEM((n_mp, own_rows, width), low), dma((2,))],
        compiler_params=pltpu.CompilerParams(vmem_limit_bytes=60 * 2**20),
    )(
        reduced, masters, sub_new, lane_new, scalar_rows, sums, layer_vector_rows, inner_biases, vector_moment,
        bias_moment, input_parts, stream,
    )
    weights = [
        part for i in (2, 6, 10) for part in (outs[i].transpose(1, 0, 2), outs[i + 1], outs[i + 2], outs[i + 3].T)
    ]
    return (outs[0].reshape(row_count, width), outs[1].T, *weights, *outs[14:])

def solution(mesh):
    in_specs = (
        P("dp", None),
        P("dp", None),
        P("dp", None),
        P("dp", None, "mp"),
        P("mp", "dp"),
        P("dp", "mp"),
        P("mp", "dp"),
        P(),
        P(),
        P("dp"),
        P(None, "mp"),
        P("mp"),
        P("dp"),
        P("dp"),
        P("mp"),
        P("mp"),
        P("dp"),
        P(),
        P(),
    )
    out_specs = (
        P("dp", None),
        P("dp", "mp"),
        P("dp", None, "mp"),
        P("mp", "dp"),
        P("dp", "mp"),
        P("mp", "dp"),
        P("dp", None, "mp"),
        P("mp", "dp"),
        P("dp", "mp"),
        P("mp", "dp"),
        P("dp", None, "mp"),
        P("mp", "dp"),
        P("dp", "mp"),
        P("mp", "dp"),
        P("dp"),
        P(None, "mp"),
        P("mp"),
        P("dp"),
        P("dp"),
        P("mp"),
        P("mp"),
        P("dp"),
        P(),
        P(),
        P(),
        P(),
        P(),
        P(),
        P(),
        P(),
    )
    fits = mesh.shape["dp"] == 8 and mesh.shape["mp"] == 4
    return jax.shard_map(shards if fits else generic, mesh=mesh, in_specs=in_specs, out_specs=out_specs, check_vma=False)
```

profile of v0, /device:TPU:0, one launch (start us, length us, event | category | flops | bytes accessed | tf_op | source)
XLA Modules:
  0.0 199.8 jit_solution(8664795016953710496)
XLA Ops:
  0.7 191.5 %shard_map.418 = (f32[3,96,768]{2,1,0:T(8,128)}, f32[3,96,768]{2,1,0:T(8,128)}, f32[16,768]{1,0:T(8,128)}, f32[8,128]{1,0:T(8,128)}, f32[8,768]{1,0:T(8,128)}, /...) custom-call(bf16[2048,768]{1,0:T(8,128)(2,1)} %tokens_in.1, bf16[2048,768]{1,0:T(8,128)(2,1)} %cot_in.1, ...), custom_call_target="tpu_custom_call" | custom-call | tf_op jit(solution)/shard_map/pallas_call | solution.py:1860
  192.2 7.4 %shard_map.419 = (bf16[4,512,768]{2,1,0:T(8,128)(2,1)}, f32[192,2048]{1,0:T(8,128)}, f32[3,96,192]{2,1,0:T(8,128)}, f32[192,96]{1,0:T(8,128)}, f32[96,768]{1,0:T...) custom-call(f32[3,96,768]{2,1,0:T(8,128)} %get-tuple-element.68.redu, ...), custom_call_target="tpu_custom_call" | custom-call | tf_op jit(solution)/shard_map/pallas_call | solution.py:1949
where the time goes:
time: 200 us
  Pallas kernels  199 us (100%)
    pallas_call x1, Pallas kernels, shards(): pl.pallas_call(functools.partial(layer_kernel, n_dp, n_mp, slot_count, ow...  192 us
    pallas_call x1, Pallas kernels, shards(): pl.pallas_call(functools.partial(update_kernel, n_dp, n_mp), out_shape=(s...  7.42 us

commit v1 on v0

--- a/solution.py
+++ b/solution.py
@@ -553,7 +553,7 @@
         d_query[here, LANES : 2 * LANES] = got[2][0].astype(low)
         return 0
 
-    lax.fori_loop(0, window // LANES, block, 0)
+    lax.fori_loop(0, window // LANES, block, 0, unroll=True)
 
 def tile_rows(i, first=0):
     return pl.ds(pl.multiple_of(first + i * LANES, LANES), LANES)
@@ -1067,11 +1067,10 @@
         for half in range(set_rows // own_rows):
             at = pl.ds(half * own_rows, own_rows)
             qkv[m, at] = (mm(normed[half, 0:own_rows], weight(0, m)) + bias[pl.ds(m, 1)]).astype(low)
-        attend(m, qkv, mixed, feat_q, feat_k, window_start, window, window // 2)
+        attend(m, qkv, mixed, feat_q, feat_k, window_start, window, window)
         return 0
 
-    project(0, 0)
-    lax.fori_loop(1, n_mp, project, 0)
+    lax.fori_loop(0, n_mp, project, 0)
     net.step(n_mp + 2)
     proj[...] = sum((mm(mixed[m], weight(0, m, pl.ds(MIX, 2 * LANES)), NT) for m in range(n_mp)), vec[6:7])
 
@@ -1090,6 +1089,8 @@
 
     def keep(group, m, lanes, block):
         w[group, m, :, :, :, lanes] = block.astype(low).reshape(*half_shape, block.shape[1])
+
+    piece = window // 1
 
     def feed(u, _):
         first_unit = n_mp + 2 * u
@@ -1098,20 +1099,16 @@
         m = net.plane(u)
 
         def rows(i, _):
-            at = tile_rows(i)
+            at = pl.ds(pl.multiple_of(i * piece, LANES // 2), piece)
             hidden = mm(normed_two[at], weight(1, m)) + bias[pl.ds(n_mp + m, 1)]
             act, slp = gelu_parts(hidden)
+            active[m, at] = act.astype(low)
             slope[m, at] = slp.astype(low)
-
-            @pl.when((i * LANES >= own_start) & (i * LANES < own_start + own_rows))
-            def _():
-                active[m, tile_rows(i - own_start // LANES)] = act.astype(low)
-
             return 0
 
-        lax.fori_loop(0, tiles, rows, 0)
+        lax.fori_loop(0, window // piece, rows, 0)
         net.step(first_unit + 3)
-        part_sum = mm(active[m], weight(2, m), NT)
+        part_sum = mm(active[m, own], weight(2, m), NT)
 
         @pl.when(u == 0)
         def _():
@@ -1122,12 +1119,14 @@
             branch[...] += part_sum
 
         def grad_rows(i, total_row):
-            at = tile_rows(i)
+            at = pl.ds(pl.multiple_of(i * piece, LANES // 2), piece)
+            row = lax.broadcasted_iota(jnp.int32, (piece, 1), 0) + i * piece
+            mine = jnp.where((row >= own_start) & (row < own_start + own_rows), 1.0, 0.0)
             dh = (mm(d_branch[at], weight(2, m)) * slope[m, at].astype(f32)).astype(low)
             slope[m, at] = dh
-            return total_row + place.is_own(i) * column_sum(dh.astype(f32))
-
-        sums[pl.ds(8 + m, 1)] = lax.fori_loop(0, tiles, grad_rows, zero_row)
+            return total_row + column_sum(mine * dh.astype(f32))
+
+        sums[pl.ds(8 + m, 1)] = lax.fori_loop(0, window // piece, grad_rows, zero_row)
         net.step(first_unit + 4)
         two_sum = mm(slope[m], weight(1, m), NT)
 
@@ -1147,7 +1146,7 @@
         net.finish(first_unit)
         net.finish(first_unit + 1)
         everything = pl.ds(0, width)
-        keep(2, m, everything, mm(turned_t[...], active[m]))
+        keep(2, m, everything, mm(turned_t[...], active[m, own]))
         back.offer(2 * u, 2, m)
         keep(1, m, everything, mm(normed_two_t[...], slope[m, own]))
         back.offer(2 * u + 1, 1, m)
@@ -1191,8 +1190,12 @@
 
     gain_two, shift_two, scale_sum, proj_sum = lax.fori_loop(0, tiles, norm_two_back, (zero_row,) * 4)
     d_proj_t[...] = d_proj[own].T
-    for u in range(n_mp):
+
+    def sent(u, _):
         net.finish(u)
+        return 0
+
+    lax.fori_loop(0, n_mp, sent, 0)
     d_normed = branch
     d_qkv = normed_two.at[pl.ds(0, own_rows)]
 
@@ -1876,7 +1879,7 @@
             held((set_rows, width), low),
             held((window, width), low),
             held((n_mp, set_rows, width), low),
-            held((n_mp, own_rows, hidden_width), low),
+            held((n_mp, window, hidden_width), low),
             held((n_mp, window, hidden_width), low),
             held((n_mp, window, 2 * LANES), low),
             held((window, width), f32),

time: 200 us -> 196 us (0.980)
  Pallas kernels: 199 us -> 195 us
    pallas_call x1, Pallas kernels: 192 us -> 187 us  [shards(): pl.pallas_call(functools.partial(layer_kernel, n_dp, n_mp, slot_count, ow...]
where the time goes in v1:
time: 196 us
  Pallas kernels  195 us (99%)
    pallas_call x1, Pallas kernels, shards(): pl.pallas_call(functools.partial(layer_kernel, n_dp, n_mp, slot_count, ow...  187 us
    pallas_call x1, Pallas kernels, shards(): pl.pallas_call(functools.partial(update_kernel, n_dp, n_mp), out_shape=(s...  7.42 us

profile of v1, /device:TPU:0, one launch (start us, length us, event | category | flops | bytes accessed | tf_op | source)
XLA Modules:
  0.0 195.7 jit_solution(2497817649907217138)
XLA Ops:
  0.7 187.4 %shard_map.418 = (f32[3,96,768]{2,1,0:T(8,128)}, f32[3,96,768]{2,1,0:T(8,128)}, f32[16,768]{1,0:T(8,128)}, f32[8,128]{1,0:T(8,128)}, f32[8,768]{1,0:T(8,128)}, /...) custom-call(bf16[2048,768]{1,0:T(8,128)(2,1)} %tokens_in.1, bf16[2048,768]{1,0:T(8,128)(2,1)} %cot_in.1, ...), custom_call_target="tpu_custom_call" | custom-call | tf_op jit(solution)/shard_map/pallas_call | solution.py:1863
  188.1 7.4 %shard_map.419 = (bf16[4,512,768]{2,1,0:T(8,128)(2,1)}, f32[192,2048]{1,0:T(8,128)}, f32[3,96,192]{2,1,0:T(8,128)}, f32[192,96]{1,0:T(8,128)}, f32[96,768]{1,0:T...) custom-call(f32[3,96,768]{2,1,0:T(8,128)} %get-tuple-element.68.redu, ...), custom_call_target="tpu_custom_call" | custom-call | tf_op jit(solution)/shard_map/pallas_call | solution.py:1952
